TPU v7x, 32 devices: a whole 2x2x4 slice. The times are simulated.
32 devices in a mesh: tm: 8 (over y, x, core), seq: 4 (over z).
Axes of the slice: x: 2, y: 2, z: 4, core: 2. Of those that a mesh axis runs over, the one named last changes fastest.
Arguments:
- window_start: float32 [384, 64], P('seq'), may hold values from -6 to 6
- latents: float32 [8, 384, 64], P('tm', 'seq'), may hold values from -6 to 6
- step_index: int32 [8], P('tm'), may hold values from 0 to 63, as said below
- sigmas: float32 [65], replicated, may hold values from 0 to 1, as said below
- w_embed: bfloat16 [64, 3072], replicated, may hold values from -0.75 to 0.75
- w_mod: bfloat16 [256, 15360], P(None, 'seq'), may hold values from -0.375 to 0.375
- w_qkv: bfloat16 [3072, 6144], P(None, 'seq'), may hold values from -0.109375 to 0.109375
- qk_gain: float32 [2, 2048], P(None, 'seq'), may hold values from 0.5 to 10, as said below
- w_out: bfloat16 [2048, 3072], P(None, 'seq'), may hold values from -0.125 to 0.125
- w_final: bfloat16 [3072, 64], P('seq'), may hold values from -0.109375 to 0.109375
Outputs:
- new_latents: float32 [8, 384, 64], P('tm', 'seq')
- error: float32 [8], P('tm')
Inputs may be any that keep to these rules, and one draw needn't show every extreme that they name: `step_index`: distinct and increasing along the window, the first 0 and the last 63. `sigmas`: decreasing, from 1 at entry 0 to 0 at entry 64. `qk_gain`: positive.
All inputs are finite; a program needn't handle non-finite values.
Results may differ from a plain program's by a relative error of at most 0.002.
Values may be sent and summed in bfloat16 or wider, within the bound.
A program may use at most 64 MiB of HBM per device.

v0:
```python
import math

import jax
import jax.numpy as jnp
from jax import lax
from jax.sharding import PartitionSpec as P

HD = 128
FREQ = 256


epsilon = 1e-06


def shifted(x, axis, by):
    length = lax.axis_size(axis)
    pairs = [(i, i + by) for i in range(length) if 0 <= i + by < length]
    return lax.ppermute(x, axis, pairs)


def carried_in(part, axis, combine, identity):
    place = lax.axis_index(axis)
    gathered = lax.all_gather(part, axis)
    state = jnp.zeros_like(part) + jnp.asarray(identity, part.dtype)

    def one(lap, state):
        return combine(state, lax.dynamic_index_in_dim(gathered, lap, 0, False))

    return lax.fori_loop(0, place, one, state)


def time_features(moment):
    half_width = FREQ // 2
    frequencies = jnp.exp(
        -math.log(10000.0) * jnp.arange(half_width, dtype=jnp.float32) / half_width
    )
    angles = moment * frequencies
    return jnp.concatenate([jnp.cos(angles), jnp.sin(angles)])


def layer_norm(values):
    average = jnp.mean(values, axis=-1, keepdims=True)
    centered = values - average
    spread = jnp.mean(centered * centered, axis=-1, keepdims=True)
    return centered * lax.rsqrt(spread + epsilon)


def rms_scale(values, gains):
    return values * lax.rsqrt(jnp.mean(values * values, axis=-1, keepdims=True) + epsilon) * gains


def project(state_low, w_embed, modulation, w_qkv, qk_gain):
    row_total = state_low.shape[0]
    block_rows = math.gcd(row_total, 512)
    heads_here = qk_gain.shape[1] // HD
    gains = qk_gain.reshape(2, heads_here, HD)

    def project_one_block(state_block):
        embedded = jnp.dot(state_block, w_embed, preferred_element_type=jnp.float32)
        shaped = (layer_norm(embedded) * (1.0 + modulation[1]) + modulation[0]).astype(jnp.bfloat16)
        mixed = jnp.dot(shaped, w_qkv, preferred_element_type=jnp.float32).reshape(
            block_rows, heads_here, 3, HD
        )
        queries = rms_scale(mixed[:, :, 0], gains[0]).astype(jnp.bfloat16)
        keys_block = rms_scale(mixed[:, :, 1], gains[1]).astype(jnp.bfloat16)
        values_block = mixed[:, :, 2].astype(jnp.bfloat16)
        return (queries, keys_block, values_block)

    blocks = lax.map(
        project_one_block,
        state_low.reshape(row_total // block_rows, block_rows, state_low.shape[1]),
    )
    return tuple((part_block.reshape(row_total, heads_here, HD) for part_block in blocks))


def attend(queries, keys_all, values_all):
    row_total = queries.shape[0]
    heads_here = queries.shape[1]
    block_rows = math.gcd(row_total, 512)

    def attend_one_block(query_block):
        scores = jnp.einsum(
            "qhd,khd->hqk", query_block, keys_all, preferred_element_type=jnp.float32
        ) * HD ** (-0.5)
        highest = jnp.max(scores, axis=-1, keepdims=True)
        raised = jnp.exp(scores - highest)
        weights = (raised / jnp.sum(raised, axis=-1, keepdims=True)).astype(jnp.bfloat16)
        return jnp.einsum(
            "hqk,khd->qhd", weights, values_all, preferred_element_type=jnp.float32
        ).astype(jnp.bfloat16)

    blocks = lax.map(
        attend_one_block, queries.reshape(row_total // block_rows, block_rows, heads_here, HD)
    )
    return blocks.reshape(row_total, heads_here * HD)


def shards(
    window_start, latents, step_index, sigmas, w_embed, w_mod, w_qkv, qk_gain, w_out, w_final
):
    seq_count = lax.axis_size("seq")
    seq_rank = lax.axis_index("seq")
    time_rank = lax.axis_index("tm")
    tok_rows = latents.shape[1]
    all_rows = tok_rows * seq_count
    width = w_embed.shape[1]
    places = jnp.arange(sigmas.shape[0], dtype=jnp.int32)
    sigma_now = jnp.sum(jnp.where(places == step_index[0], sigmas, jnp.zeros_like(sigmas)))
    sigma_next = jnp.sum(jnp.where(places == step_index[0] + 1, sigmas, jnp.zeros_like(sigmas)))
    step_size = sigma_next - sigma_now
    features = time_features(1000.0 * sigma_now).astype(jnp.bfloat16)[None, :]
    mod_piece = jnp.dot(features, w_mod, preferred_element_type=jnp.float32)
    earlier = shifted(latents, "tm", 1)
    state_own = jnp.where(time_rank == 0, window_start, earlier[0])
    state_all, mod_rows = (
        lax.all_gather(state_own, "seq", axis=0, tiled=True),
        lax.all_gather(mod_piece, "seq", axis=0, tiled=True),
    )
    modulation = mod_rows.reshape(5, width)
    state_low = state_all.astype(jnp.bfloat16)
    queries, keys_all, values_all = project(state_low, w_embed, modulation, w_qkv, qk_gain)
    outputs = attend(queries, keys_all, values_all)
    col_count = w_out.shape[1]
    col_first = seq_rank * col_count
    own_heads = lax.all_to_all(outputs, "seq", split_axis=0, concat_axis=1, tiled=True)
    attended = jnp.dot(
        lax.all_gather(own_heads, "seq", axis=0, tiled=True),
        w_out,
        preferred_element_type=jnp.float32,
    )
    embed_cols = jnp.dot(
        state_low,
        lax.dynamic_slice_in_dim(w_embed, col_first, col_count, 1),
        preferred_element_type=jnp.float32,
    )
    mod_cols = lax.dynamic_slice_in_dim(modulation, col_first, col_count, 1)
    hidden = embed_cols + mod_cols[2] * attended
    row_sums, row_squares = lax.psum(
        (jnp.sum(hidden, axis=1), jnp.sum(hidden * hidden, axis=1)), "seq"
    )
    average = row_sums / width
    spread = row_squares / width - average * average
    centered = (hidden - average[:, None]) * lax.rsqrt(spread + epsilon)[:, None]
    normed = (centered * (1.0 + mod_cols[4]) + mod_cols[3]).astype(jnp.bfloat16)
    drift = lax.psum_scatter(
        jnp.dot(normed, w_final, preferred_element_type=jnp.float32).astype(jnp.bfloat16),
        "seq",
        scatter_dimension=0,
        tiled=True,
    ).astype(jnp.float32)
    increment = step_size * drift + jnp.where(
        time_rank == 0, window_start, jnp.zeros_like(window_start)
    )
    increment = increment[None]

    def add_terms(earlier_sum, later_sum):
        return earlier_sum + later_sum

    before = carried_in(increment, "tm", add_terms, jnp.zeros_like(increment))
    new_latents = before + increment
    difference = new_latents - latents
    total_square = lax.psum(jnp.sum(difference * difference), "seq")
    error = (total_square / (all_rows * latents.shape[2])).reshape(1)
    return (new_latents, error)


def solution(mesh):
    placed = (
        P("seq", None),
        P("tm", "seq", None),
        P("tm"),
        P(),
        P(),
        P(None, "seq"),
        P(None, "seq"),
        P(None, "seq"),
        P(None, "seq"),
        P("seq", None),
    )
    return jax.shard_map(
        shards,
        mesh=mesh,
        in_specs=placed,
        out_specs=(P("tm", "seq", None), P("tm")),
        check_vma=False,
    )
```

profile of v0, /device:TPU:6, one launch (start us, length us, event | category | flops | bytes accessed | tf_op | source)
XLA Modules:
  0.0 215.7 jit_solution(2972329266579261484)
XLA Ops:
  8.2 2.0 collective-permute-start
  10.9 1.3 fusion.36
  12.9 1.9 convolution_bitcast_fusion
  14.8 13.4 %all-gather.3 = f32[4,1,3840]{2,1,0:T(1,128)S(1)} all-gather(f32[1,1,3840]{2,1,0:T(1,128)S(1)} %convolution_bitcast_fusion), channel_id=2, replica_groups=mesh['tm'=8,'seq'=4] {'seq'}, dimensions={0}, use_global_device_ids=true | all-gather | bytes 76800 | tf_op jit(solution)/shard_map/all_gather | solution.py:117
  29.1 13.1 %all-gather.2 = bf16[4,96,64]{1,2,0:T(8,128)(2,1)S(1)} all-gather(bf16[1,96,64]{1,2,0:T(8,128)(2,1)S(1)} %fusion.34), channel_id=1, replica_groups=mesh['tm'=8,'seq'=4] {'seq'}, dimensions={0}, use_global_device_ids=true | all-gather | bytes 61440 | tf_op jit(solution)/shard_map/all_gather | solution.py:116
  43.0 42.2 %while.34 = (s32[]{:T(128)}, bf16[3,128,4,128]{1,3,2,0:T(8,128)(2,1)}, bf16[3,128,4,128]{3,1,0,2:T(8,128)(2,1)}, bf16[3,128,4,128]{3,1,0,2:T(8,128)(2,1)}, bf16[...) while((s32[]{:T(128)}, ...), condition=%wide.region_7.8_spmd, body=%wide.region_2.7_spmd.sunk | while | flops 1262489728 | bytes 21244032 | solution.py:69
  43.0 1.4 fusion.68
  45.7 6.5 %fusion.69 = f32[128,1536]{0,1:T(8,128)S(1)} fusion(bf16[3072,1536]{1,0:T(8,128)(2,1)} %get-tuple-element.387, f32[128,3072]{1,0:T(8,128)S(1)} %get-tuple-element.339, f32[3072]{0:T(1024)S(1)} %bitcast.116, f32[3072]{0:T(1024)S(1)} %bitcast.115, f32[128]{0:T(128)S(1)} %add_rsqrt_fusion.7, f32[128]{0:T(128)S(1)} %broadcast_multiply_fusion.3), kind=kOutput, calls=%fused_computation.2.clone.1 | convolution fusion | flops 1209925632 | bytes 11822080 | tf_op jit(solution)/shard_map/while/body/eval_jaxpr/dot_general | solution.py:61
  55.3 1.7 fusion.70
  57.0 1.4 fusion.68
  59.8 6.5 %fusion.69 = f32[128,1536]{0,1:T(8,128)S(1)} fusion(bf16[3072,1536]{1,0:T(8,128)(2,1)} %get-tuple-element.387, f32[128,3072]{1,0:T(8,128)S(1)} %get-tuple-element.339, f32[3072]{0:T(1024)S(1)} %bitcast.116, f32[3072]{0:T(1024)S(1)} %bitcast.115, f32[128]{0:T(128)S(1)} %add_rsqrt_fusion.7, f32[128]{0:T(128)S(1)} %broadcast_multiply_fusion.3), kind=kOutput, calls=%fused_computation.2.clone.1 | convolution fusion | flops 1209925632 | bytes 11822080 | tf_op jit(solution)/shard_map/while/body/eval_jaxpr/dot_general | solution.py:61
  69.3 1.7 fusion.70
  71.1 1.4 fusion.68
  73.9 6.5 %fusion.69 = f32[128,1536]{0,1:T(8,128)S(1)} fusion(bf16[3072,1536]{1,0:T(8,128)(2,1)} %get-tuple-element.387, f32[128,3072]{1,0:T(8,128)S(1)} %get-tuple-element.339, f32[3072]{0:T(1024)S(1)} %bitcast.116, f32[3072]{0:T(1024)S(1)} %bitcast.115, f32[128]{0:T(128)S(1)} %add_rsqrt_fusion.7, f32[128]{0:T(128)S(1)} %broadcast_multiply_fusion.3), kind=kOutput, calls=%fused_computation.2.clone.1 | convolution fusion | flops 1209925632 | bytes 11822080 | tf_op jit(solution)/shard_map/while/body/eval_jaxpr/dot_general | solution.py:61
  83.4 1.7 fusion.70
  85.1 14.1 %while.35 = (s32[]{:T(128)}, bf16[3,128,4,128]{3,2,1,0:T(4,128)(2,1)}, bf16[3,128,4,128]{1,3,2,0:T(8,128)(2,1)}, bf16[384,4,128]{2,0,1:T(8,128)(2,1)}, bf16[384,4,128]{2,0,1:T(8,128)(2,1)}, /*index=5*/s32[]{:T(128)}) while((s32[]{:T(128)}, bf16[3,128,4,128]{3,2,1,0:T(4,128)(2,1)}, bf16[3,128,4,128]{1,3,2,0:T(8,128)(2,1)}, ...), condition=%wide.region_11.12_spmd, body=%wide.region_8.11_spmd.sunk | while | flops 101712256 | bytes 2888773 | solution.py:92
  85.1 2.4 %fusion.76 = (f32[4,128]{1,0:T(4,128)S(1)}, f32[4,128,384]{2,1,0:T(8,128)}) fusion(bf16[384,4,128]{2,0,1:T(8,128)(2,1)} %get-tuple-element.405, bf16[3,128,4,128]{1,3,2,0:T(8,128)(2,1)} %get-tuple-element.404, s32[]{:T(128)} %get-tuple-element.396), kind=kOutput, calls=%fused_computation.78.clone.1 | convolution fusion | flops 50921856 | bytes 1313280 | tf_op jit(solution)/shard_map/while/body/eval_jaxpr/sub | solution.py:86
  87.5 1.6 fusion.77
  89.8 2.4 %fusion.76 = (f32[4,128]{1,0:T(4,128)S(1)}, f32[4,128,384]{2,1,0:T(8,128)}) fusion(bf16[384,4,128]{2,0,1:T(8,128)(2,1)} %get-tuple-element.405, bf16[3,128,4,128]{1,3,2,0:T(8,128)(2,1)} %get-tuple-element.404, s32[]{:T(128)} %get-tuple-element.396), kind=kOutput, calls=%fused_computation.78.clone.1 | convolution fusion | flops 50921856 | bytes 1313280 | tf_op jit(solution)/shard_map/while/body/eval_jaxpr/sub | solution.py:86
  92.2 1.6 fusion.77
  94.5 2.4 %fusion.76 = (f32[4,128]{1,0:T(4,128)S(1)}, f32[4,128,384]{2,1,0:T(8,128)}) fusion(bf16[384,4,128]{2,0,1:T(8,128)(2,1)} %get-tuple-element.405, bf16[3,128,4,128]{1,3,2,0:T(8,128)(2,1)} %get-tuple-element.404, s32[]{:T(128)} %get-tuple-element.396), kind=kOutput, calls=%fused_computation.78.clone.1 | convolution fusion | flops 50921856 | bytes 1313280 | tf_op jit(solution)/shard_map/while/body/eval_jaxpr/sub | solution.py:86
  96.9 1.6 fusion.77
  100.4 13.3 %all_to_all.19 = bf16[4,96,512]{2,1,0:T(8,128)(2,1)S(1)} all-to-all(bf16[4,96,512]{2,1,0:T(8,128)(2,1)S(1)} %all_to_all.14), channel_id=1, replica_groups=mesh['tm'=8,'seq'=4] {'seq'}, dimensions={0} | all-to-all | bytes 786432 | tf_op jit(solution)/shard_map/all_to_all | solution.py:125
  116.5 34.1 %all-gather.7.cloned.1.call-done = bf16[384,2048]{1,0:T(8,128)(2,1)} async-done(((bf16[96,2048]{1,0:T(8,128)(2,1)}), bf16[384,2048]{1,0:T(8,128)(2,1)}) %all-gather.7.cloned.1.call-update) | async-done | bytes 1572880 | tf_op jit(solution)/shard_map/all_gather | solution.py:127
  150.5 2.8 %convolution_multiply_fusion.1 = f32[384,768]{1,0:T(8,128)S(1)} fusion(bf16[384,2048]{1,0:T(8,128)(2,1)} %all-gather.7.cloned.1.call-done, bf16[2048,768]{1,0:T(8,128)(2,1)S(1)} %copy-done, f32[768]{0:T(1024)S(1)} %get-tuple-element.165), kind=kOutput, calls=%fused_computation.49 | convolution fusion | flops 1208254464 | bytes 5901312 | tf_op jit(solution)/shard_map/dot_general | solution.py:126
  153.4 2.3 %fusion.39 = (f32[384]{0:T(512)S(1)}, f32[384]{0:T(512)S(1)}, f32[384,768]{1,0:T(8,128)}) fusion(f32[384,768]{1,0:T(8,128)S(1)} %convolution_multiply_fusion.1, bf16[384,64]{0,1:T(8,128)(2,1)S(1)} %reshape.130, bf16[64,3072]{1,0:T(8,128)(2,1)} %param.20, s32[]{:T(128)S(6)} %select_n.31), kind=kOutput, calls=%fused_computation.76 | convolution fusion | flops 38927616 | bytes 2509828 | tf_op jit(solution)/shard_map/dot_general | solution.py:131
  155.7 9.6 %all-reduce = (f32[384]{0:T(512)S(1)}, f32[384]{0:T(512)S(1)}) all-reduce(f32[384]{0:T(512)S(1)} %get-tuple-element.163, f32[384]{0:T(512)S(1)} %get-tuple-element.162), channel_id=1, replica_groups=mesh['tm'=8,'seq'=4] {'seq'}, use_global_device_ids=true, to_apply=%region_15.16 | all-reduce | flops 768 | bytes 6144 | tf_op jit(solution)/shard_map/psum | solution.py:138
  165.3 1.7 convolution_convert_fusion.1
  168.9 16.4 %reduce-scatter.4.cloned.1.call-done = bf16[96,64]{1,0:T(8,128)(2,1)} async-done(((bf16[384,64]{1,0:T(8,128)(2,1)}), bf16[96,64]{1,0:T(8,128)(2,1)}) %reduce-scatter.4.cloned.1.call-update) | async-done | bytes 12304
  186.2 8.4 %all-gather.4 = f32[8,96,64]{1,2,0:T(8,128)S(1)} all-gather(f32[1,96,64]{1,2,0:T(8,128)S(1)} %add_bitcast_fusion), channel_id=3, replica_groups=mesh['tm'=8,'seq'=4] {'tm'}, dimensions={0}, use_global_device_ids=true | all-gather | bytes 221184 | tf_op jit(solution)/shard_map/all_gather | solution.py:23
  195.6 2.0 multiply_reduce_fusion.4
  197.6 9.5 %psum.23 = f32[]{:T(128)} all-reduce(f32[]{:T(128)} %get-tuple-element.207), channel_id=1, replica_groups=mesh['tm'=8,'seq'=4] {'seq'}, use_global_device_ids=true, to_apply=%region_20.21 | all-reduce | flops 1 | bytes 8 | tf_op jit(solution)/shard_map/psum | solution.py:162
  (110 shorter events, 24.9 us)
Async XLA Ops:
  7.2 143.4 %copy-start = (bf16[2048,768]{1,0:T(8,128)(2,1)S(1)}, bf16[2048,768]{1,0:T(8,128)(2,1)}, u32[]{:S(2)}) copy-start(bf16[2048,768]{1,0:T(8,128)(2,1)} %param.24) | copy-start | bytes 9437188
  7.2 21.9 %copy-start.6 = (f32[2,512]{1,0:T(2,128)S(1)}, f32[2,512]{1,0:T(2,128)}, u32[]{:S(2)}) copy-start(f32[2,512]{1,0:T(2,128)} %param.23) | copy-start | bytes 12292
  7.2 21.9 %copy-start.4 = (f32[96,64]{0,1:T(8,128)S(1)}, f32[96,64]{0,1:T(8,128)}, u32[]{:S(2)}) copy-start(f32[96,64]{0,1:T(8,128)} %param.16) | copy-start | bytes 73732
  7.2 143.3 %all-gather.7.cloned.1.call-start = ((), (), s32[]{:S(2)}) async-start(), calls=%async_computation.2 | async-start | bytes 1966080 | tf_op jit(solution)/shard_map/all_gather | solution.py:127
  8.2 20.9 %collective-permute-start = (bf16[1,96,64]{1,2,0:T(8,128)(2,1)S(1)}, bf16[1,96,64]{1,2,0:T(8,128)(2,1)S(1)}, u32[]{:S(2)}, u32[]{:S(2)}) collective-permute-start(bf16[1,96,64]{1,2,0:T(8,128)(2,1)S(1)} %convert.20), channel_id=1, source_target_pairs={{0,4},{4,8},{8,12},{12,16},{16,20},{20,24},{24,28},{1,5},{5,9},{9,... | collective-permute-start | bytes 36872 | tf_op jit(solution)/shard_map/ppermute | solution.py:18
  42.2 0.7 copy-start.2
  52.3 0.9 copy-start.1
  66.3 0.9 copy-start.1
  80.4 0.9 copy-start.1
  114.5 70.9 %reduce-scatter.4.cloned.1.call-start = ((), (), s32[]{:S(2)}) async-start(), calls=%async_computation.3 | async-start | bytes 122880
  153.3 11.9 %copy-start.7 = (bf16[768,64]{0,1:T(8,128)(2,1)S(1)}, bf16[768,64]{0,1:T(8,128)(2,1)}, u32[]{:S(2)}) copy-start(bf16[768,64]{0,1:T(8,128)(2,1)} %param.25) | copy-start | bytes 294916
  153.3 32.8 %copy-start.5 = (f32[96,64]{0,1:T(8,128)S(1)}, f32[96,64]{0,1:T(8,128)}, u32[]{:S(2)}) copy-start(f32[96,64]{0,1:T(8,128)} %param.16) | copy-start | bytes 73732
  186.2 8.4 %copy-start.3 = (f32[1,96,64]{1,2,0:T(8,128)}, f32[1,96,64]{1,2,0:T(8,128)S(1)}, u32[]{:S(2)}) copy-start(f32[1,96,64]{1,2,0:T(8,128)S(1)} %add_bitcast_fusion) | copy-start | bytes 73732
Sparse Core Ops, SparseCore 0:
  114.6 35.9 all-gather.6
  167.9 17.4 reduce-scatter.3
where the time goes:
time: 218 us; the launch traced here: 216 us
  blocking collectives  67.3 us (31%)
  waiting for transfers between devices  50.5 us (23%)
  matrix products  44.3 us (20%)
  between operations  18.4 us (8%)
  local copies, waits for them, and re-layouts  17.2 us (8%)
  other arithmetic  15.3 us (7%)
    all_gather x1, waiting for transfers between devices, shards(): lax.all_gather(own_heads, 'seq', axis=0, tiled=True)  34.1 us
    dot_general x3, matrix products, project_one_block(): jnp.dot(shaped, w_qkv, preferred_element_type=jnp.float32)  19.5 us
    unnamed x3, waiting for transfers between devices  16.4 us
    all_gather x1, blocking collectives, shards(): lax.all_gather(mod_piece, 'seq', axis=0, tiled=True)  13.4 us
    all_to_all x1, blocking collectives, shards(): lax.all_to_all(outputs, 'seq', split_axis=0, concat_axis=1, tiled=True)  13.3 us
    all_gather x1, blocking collectives, shards(): lax.all_gather(state_own, 'seq', axis=0, tiled=True)  13.1 us
    psum x1, blocking collectives, shards(): lax.psum((jnp.sum(hidden, axis=1), jnp.sum(hidden * hidden, axis=1)), 'seq')  9.59 us
    psum x1, blocking collectives, shards(): total_square = lax.psum(jnp.sum(difference * difference), 'seq')  9.48 us
  transfers between devices with their start and end apart: 3, of which 2 were waited for; matrix products, arithmetic and copies ran while one was open for 3% of the time, Pallas kernels for 0%

commit v1 on v0

--- a/solution.py
+++ b/solution.py
@@ -1,8 +1,11 @@
+import functools
 import math
 
 import jax
 import jax.numpy as jnp
 from jax import lax
+from jax.experimental import pallas as pl
+from jax.experimental.pallas import tpu as pltpu
 from jax.sharding import PartitionSpec as P
 
 HD = 128
@@ -164,6 +167,417 @@
     return (new_latents, error)
 
 
+MESH = pl.DeviceIdType.MESH
+
+
+def block_kernel(
+    dims, index_ref, sigmas_ref, start_ref, latents_ref, gains_ref, w_embed_hbm, w_mod_hbm,
+    w_qkv_hbm, w_out_hbm, w_final_hbm, new_ref, error_ref,
+    w_embed, w_mod, w_qkv, w_out, w_final, state_out, state, mod, embedded, shaped, attended, total,
+    part_out, parts, terms, squares,
+    load_sem, qkv_sem, state_send, state_recv, mod_send, mod_recv, right_send, left_send, att_recv,
+    part_send, part_recv, term_send, term_recv, square_send, square_recv,
+):
+    times, n, heads, rows, width, chan = dims
+    cols = width // n
+    all_rows = rows * n
+    me_t, me = lax.axis_index("tm"), lax.axis_index("seq")
+    next_t, prev_t = lax.rem(me_t + 1, times), lax.rem(me_t + times - 1, times)
+
+    barrier = pltpu.get_barrier_semaphore()
+    peers = []
+    for k in range(1, n):
+        other = lax.rem(me + k, n)
+        peers += [(me_t, other), (next_t, other), (prev_t, other)]
+    for k in range(1, times):
+        peers.append((lax.rem(me_t + k, times), me))
+    for peer in peers:
+        pl.semaphore_signal(barrier, inc=1, device_id=peer, device_id_type=MESH)
+
+    load_mod = pltpu.make_async_copy(w_mod_hbm, w_mod, load_sem.at[0])
+    load_embed = pltpu.make_async_copy(w_embed_hbm, w_embed, load_sem.at[1])
+    load_final = pltpu.make_async_copy(w_final_hbm, w_final, load_sem.at[2])
+    load_out = pltpu.make_async_copy(w_out_hbm, w_out, load_sem.at[3])
+    load_mod.start()
+    load_embed.start()
+    for h in range(heads):
+        pltpu.make_async_copy(
+            w_qkv_hbm.at[:, pl.ds(h * 3 * HD, 3 * HD)], w_qkv.at[h], qkv_sem.at[h]
+        ).start()
+    load_final.start()
+    load_out.start()
+
+    state_out[...] = jnp.where(me_t == times - 1, start_ref[...], latents_ref[0]).astype(jnp.bfloat16)
+
+    sigma_now = sigmas_ref[index_ref[0]]
+    step_size = sigmas_ref[index_ref[0] + 1] - sigma_now
+    place = lax.broadcasted_iota(jnp.int32, (16, FREQ // 2), 1).astype(jnp.float32)
+    angles = (1000.0 * sigma_now) * jnp.exp(place * (-math.log(10000.0) / (FREQ // 2)))
+    features = jnp.concatenate([jnp.cos(angles), jnp.sin(angles)], axis=1).astype(jnp.bfloat16)
+
+    pl.semaphore_wait(barrier, len(peers))
+
+    def remote(source, target, send, recv, device):
+        return pltpu.make_async_remote_copy(
+            src_ref=source, dst_ref=target, send_sem=send, recv_sem=recv,
+            device_id=device, device_id_type=MESH,
+        )
+
+    def state_copy(slot, target):
+        return remote(
+            state_out, state.at[slot], state_send.at[target], state_recv.at[slot], (next_t, target)
+        )
+
+    for k in range(n):
+        state_copy(me, k).start()
+
+    def mod_copy(owner, k):
+        held = mod.at[pl.ds(owner * 5, 5)]
+        return remote(
+            held, held, mod_send.at[k], mod_recv.at[owner], (me_t, lax.rem(me + k, n))
+        )
+
+    load_mod.wait()
+    for i in range(5):
+        piece = jnp.dot(
+            features, w_mod[:, i * cols : (i + 1) * cols], preferred_element_type=jnp.float32
+        )
+        mod[me * 5 + i] = piece[0:1]
+    for k in range(1, n):
+        mod_copy(me, k).start()
+
+    load_embed.wait()
+    for k in range(n):
+        state_copy(k, 0).wait_recv()
+    state_low = state[...].reshape(all_rows, chan)
+    sums = jnp.zeros((all_rows, 1), jnp.float32)
+    for j in range(n):
+        tile = jnp.dot(
+            state_low, w_embed[:, j * cols : (j + 1) * cols], preferred_element_type=jnp.float32
+        )
+        embedded[:, j * cols : (j + 1) * cols] = tile
+        sums = sums + jnp.sum(tile, axis=1, keepdims=True)
+    total[:, 0:1] = sums / width
+    for k in range(1, n):
+        mod_copy(lax.rem(me + k, n), k).wait_recv()
+
+    block = 32
+
+    def shape_rows(i, carry):
+        at = pl.ds(pl.multiple_of(i * block, block), block)
+        average = total[at, 0:1]
+        spread = jnp.zeros((block, 1), jnp.float32)
+        for j in range(n):
+            centered = embedded[at, j * cols : (j + 1) * cols] - average
+            spread = spread + jnp.sum(centered * centered, axis=1, keepdims=True)
+        scale = lax.rsqrt(spread / width + epsilon)
+        for j in range(n):
+            centered = embedded[at, j * cols : (j + 1) * cols] - average
+            value = centered * scale * (1.0 + mod[n + j]) + mod[j]
+            shaped[at, j * cols : (j + 1) * cols] = value.astype(jnp.bfloat16)
+        return carry
+
+    lax.fori_loop(0, all_rows // block, shape_rows, 0)
+
+    def att_copy(owner, h, right):
+        slot = owner * heads + h
+        sems = right_send if right else left_send
+        held = attended.at[slot]
+        return remote(
+            held, held, sems.at[slot], att_recv.at[slot], (me_t, me + 1 if right else me - 1)
+        )
+
+    def one_head(h, carry):
+        pltpu.make_async_copy(
+            w_qkv_hbm.at[:, pl.ds(0, 3 * HD)], w_qkv.at[h], qkv_sem.at[h]
+        ).wait()
+        mixed = jnp.dot(shaped[...], w_qkv[h], preferred_element_type=jnp.float32)
+        here = pl.ds(pl.multiple_of(h * HD, HD), HD)
+        queries = rms_scale(mixed[:, :HD], gains_ref[0:1, here]).astype(jnp.bfloat16)
+        keys = rms_scale(mixed[:, HD : 2 * HD], gains_ref[1:2, here]).astype(jnp.bfloat16)
+        values = mixed[:, 2 * HD :].astype(jnp.bfloat16)
+        scores = lax.dot_general(
+            queries, keys, (((1,), (1,)), ((), ())), preferred_element_type=jnp.float32
+        )
+        raised = jnp.exp((scores - jnp.max(scores, axis=1, keepdims=True)) * HD ** (-0.5))
+        weights = raised * (1.0 / jnp.sum(raised, axis=1, keepdims=True))
+        attended[me * heads + h] = jnp.dot(
+            weights.astype(jnp.bfloat16), values, preferred_element_type=jnp.float32
+        ).astype(jnp.bfloat16)
+
+        @pl.when(me < n - 1)
+        def _():
+            att_copy(me, h, True).start()
+
+        @pl.when(me > 0)
+        def _():
+            att_copy(me, h, False).start()
+
+        return carry
+
+    lax.fori_loop(0, heads, one_head, 0)
+
+    load_final.wait()
+    load_out.wait()
+
+    def multiply(slot):
+        at = pl.ds(pl.multiple_of(slot * HD, HD), HD)
+        return jnp.dot(attended[slot], w_out[at, :], preferred_element_type=jnp.float32)
+
+    total[...] = jnp.zeros((all_rows, cols), jnp.float32)
+
+    def own_head(h, carry):
+        total[...] += multiply(me * heads + h)
+        return carry
+
+    lax.fori_loop(0, heads, own_head, 0)
+
+    gate, shift, scale = mod[2 * n + me], mod[3 * n + me], 1.0 + mod[4 * n + me]
+    final = w_final[...]
+    row = lax.broadcasted_iota(jnp.int32, (16, cols), 0)
+
+    def high(x):
+        return x.astype(jnp.bfloat16).astype(jnp.float32)
+
+    stacked = jnp.where(
+        row == 0,
+        high(scale),
+        jnp.where(row == 1, scale - high(scale), jnp.where(row == 2, high(shift), shift - high(shift))),
+    )
+    sides = jnp.dot(stacked.astype(jnp.bfloat16), final, preferred_element_type=jnp.float32)
+    side_row = lax.broadcasted_iota(jnp.int32, (8, chan), 0)
+    sides = jnp.where(
+        side_row == 0,
+        sides[0:1] + sides[1:2],
+        jnp.where(side_row == 1, sides[2:3] + sides[3:4], 0.0),
+    )
+    sides = jnp.concatenate([sides, jnp.zeros((8, 128 - chan), jnp.float32)], axis=1)
+
+    def arrived(step, carry):
+        far, h = step // heads + 1, lax.rem(step, heads)
+
+        @pl.when(me - far >= 0)
+        def _():
+            att_copy(me - far, h, True).wait_recv()
+
+            @pl.when(me < n - 1)
+            def _():
+                att_copy(me - far, h, True).start()
+
+        @pl.when(me + far < n)
+        def _():
+            att_copy(me + far, h, False).wait_recv()
+
+            @pl.when(me > 0)
+            def _():
+                att_copy(me + far, h, False).start()
+
+        @pl.when(me - far >= 0)
+        def _():
+            total[...] += multiply((me - far) * heads + h)
+
+        @pl.when(me + far < n)
+        def _():
+            total[...] += multiply((me + far) * heads + h)
+
+        return carry
+
+    lax.fori_loop(0, (n - 1) * heads, arrived, 0)
+
+    my_cols = pl.ds(pl.multiple_of(me * cols, cols), cols)
+    lane = lax.broadcasted_iota(jnp.int32, (rows, 128 - chan), 1)
+
+    def part_of(owner):
+        at = pl.ds(pl.multiple_of(owner * rows, rows), rows)
+        hidden = embedded[at, my_cols] + gate * total[at, :]
+        sums = jnp.sum(hidden, axis=1, keepdims=True)
+        square_sums = jnp.sum(hidden * hidden, axis=1, keepdims=True)
+        scaled = hidden * scale
+        upper = scaled.astype(jnp.bfloat16)
+        lower = (scaled - upper.astype(jnp.float32)).astype(jnp.bfloat16)
+        product = jnp.dot(upper, final, preferred_element_type=jnp.float32) + jnp.dot(
+            lower, final, preferred_element_type=jnp.float32
+        )
+        stats = jnp.where(lane == 0, sums, jnp.where(lane == 1, square_sums, 0.0))
+        return jnp.concatenate([product, stats], axis=1)
+
+    def part_copy(k, source, owner):
+        return remote(
+            part_out.at[k - 1], parts.at[source], part_send.at[k - 1], part_recv.at[source],
+            (me_t, owner),
+        )
+
+    for k in range(1, n):
+        owner = lax.rem(me + k, n)
+        part_out[k - 1, :rows] = part_of(owner)
+        part_out[k - 1, rows:] = sides
+        part_copy(k, me, owner).start()
+    parts[me, :rows] = part_of(me)
+    parts[me, rows:] = sides
+    for k in range(1, n):
+        source = lax.rem(me + k, n)
+        part_copy(k, source, source).wait_recv()
+    summed = parts[0]
+    for k in range(1, n):
+        summed = summed + parts[k]
+    average = summed[:rows, chan : chan + 1] / width
+    spread = summed[:rows, chan + 1 : chan + 2] / width - average * average
+    drift = (summed[:rows, :chan] - average * summed[rows : rows + 1, :chan]) * lax.rsqrt(
+        spread + epsilon
+    ) + summed[rows + 1 : rows + 2, :chan]
+    increment = step_size * drift
+    half = rows // 2
+    packed = jnp.concatenate([increment[:half], increment[half:]], axis=1)
+    terms[me_t] = packed
+
+    def term_copy(source, target):
+        return remote(
+            terms.at[source], terms.at[source], term_send.at[target], term_recv.at[source],
+            (target, me),
+        )
+
+    for k in range(1, times):
+
+        @pl.when(me_t + k < times)
+        def _():
+            term_copy(me_t, me_t + k).start()
+
+    for k in range(1, times):
+
+        @pl.when(me_t - k >= 0)
+        def _():
+            term_copy(me_t - k, me_t).wait_recv()
+
+        @pl.when(me_t - k < 0)
+        def _():
+            terms[me_t - k + times] = jnp.zeros((half, 128), jnp.float32)
+
+    before = terms[0]
+    for k in range(1, times):
+        before = before + terms[k]
+    change = jnp.concatenate([before[:, :chan], before[:, chan:]], axis=0)
+    updated = start_ref[...] + change
+    new_ref[0] = updated
+    difference = updated - latents_ref[0]
+    squares[me] = jnp.broadcast_to(jnp.sum(difference * difference), (8, 128))
+
+    def square_copy(source, k):
+        return remote(
+            squares.at[source], squares.at[source], square_send.at[k], square_recv.at[source],
+            (me_t, lax.rem(me + k, n)),
+        )
+
+    for k in range(1, n):
+        square_copy(me, k).start()
+
+    for k in range(n):
+        state_copy(me, k).wait_send()
+    for k in range(1, n):
+        mod_copy(me, k).wait_send()
+        part_copy(k, me, lax.rem(me + k, n)).wait_send()
+    for k in range(1, times):
+
+        @pl.when(me_t + k < times)
+        def _():
+            term_copy(me_t, me_t + k).wait_send()
+
+    def all_sent(slot, carry):
+        owner, h = slot // heads, lax.rem(slot, heads)
+
+        @pl.when((owner <= me) & (me < n - 1))
+        def _():
+            att_copy(owner, h, True).wait_send()
+
+        @pl.when((owner >= me) & (me > 0))
+        def _():
+            att_copy(owner, h, False).wait_send()
+
+        return carry
+
+    lax.fori_loop(0, n * heads, all_sent, 0)
+    for k in range(1, n):
+        square_copy(me, k).wait_send()
+        square_copy(lax.rem(me + k, n), k).wait_recv()
+    square_total = squares[0]
+    for k in range(1, n):
+        square_total = square_total + squares[k]
+    error_ref[0] = jnp.max(square_total) / (all_rows * chan)
+
+
+def fused(times, n, *args):
+    (window_start, latents, step_index, sigmas, w_embed, w_mod, w_qkv, qk_gain, w_out, w_final) = args
+    rows, chan = window_start.shape
+    width = w_embed.shape[1]
+    heads = qk_gain.shape[1] // HD
+    cols = width // n
+    low, wide = jnp.bfloat16, jnp.float32
+    vmem, smem, hbm = (
+        pl.BlockSpec(memory_space=space) for space in (pltpu.VMEM, pltpu.SMEM, pl.ANY)
+    )
+    dma = pltpu.SemaphoreType.DMA
+    flops = 2 * rows * n * (width * heads * 3 * HD + n * heads * HD * cols)
+    return pl.pallas_call(
+        functools.partial(block_kernel, (times, n, heads, rows, width, chan)),
+        out_shape=(
+            jax.ShapeDtypeStruct(latents.shape, wide),
+            jax.ShapeDtypeStruct((1,), wide),
+        ),
+        in_specs=[smem, smem, vmem, vmem, vmem, hbm, hbm, hbm, hbm, hbm],
+        out_specs=(vmem, smem),
+        scratch_shapes=[
+            pltpu.VMEM(w_embed.shape, low),
+            pltpu.VMEM(w_mod.shape, low),
+            pltpu.VMEM((heads, width, 3 * HD), low),
+            pltpu.VMEM(w_out.shape, low),
+            pltpu.VMEM(w_final.shape, low),
+            pltpu.VMEM((rows, chan), low),
+            pltpu.VMEM((n, rows, chan), low),
+            pltpu.VMEM((5 * n, 1, cols), wide),
+            pltpu.VMEM((rows * n, width), wide),
+            pltpu.VMEM((rows * n, width), low),
+            pltpu.VMEM((n * heads, rows * n, HD), low),
+            pltpu.VMEM((rows * n, cols), wide),
+            pltpu.VMEM((n - 1, rows + 8, 128), wide),
+            pltpu.VMEM((n, rows + 8, 128), wide),
+            pltpu.VMEM((times, rows // 2, 128), wide),
+            pltpu.VMEM((n, 8, 128), wide),
+            dma((4,)),
+            dma((heads,)),
+            dma((n,)),
+            dma((n,)),
+            dma((n,)),
+            dma((n,)),
+            dma((n * heads,)),
+            dma((n * heads,)),
+            dma((n * heads,)),
+            dma((n - 1,)),
+            dma((n,)),
+            dma((times,)),
+            dma((times,)),
+            dma((n,)),
+            dma((n,)),
+        ],
+        compiler_params=pltpu.CompilerParams(
+            collective_id=0, has_side_effects=True, vmem_limit_bytes=56 * 2**20
+        ),
+        cost_estimate=pl.CostEstimate(flops=flops, bytes_accessed=16 * 2**20, transcendentals=0),
+    )(step_index, sigmas, window_start, latents, qk_gain, w_embed, w_mod, w_qkv, w_out, w_final)
+
+
+def fits(times, n, args):
+    rows, chan = args[0].shape
+    cols = args[4].shape[1] // n
+    small = rows * n * args[4].shape[1] <= 384 * 3072
+    return times > 2 and n > 1 and cols % 128 == 0 and rows % 32 == 0 and chan == 64 and small
+
+
+def device_part(*args):
+    times, n = lax.axis_size("tm"), lax.axis_size("seq")
+    if fits(times, n, args):
+        return fused(times, n, *args)
+    return shards(*args)
+
+
 def solution(mesh):
     placed = (
         P("seq", None),
@@ -178,7 +592,7 @@
         P("seq", None),
     )
     return jax.shard_map(
-        shards,
+        device_part,
         mesh=mesh,
         in_specs=placed,
         out_specs=(P("tm", "seq", None), P("tm")),

time: 218 us -> 68.1 us (0.31)
  blocking collectives: 67.3 us -> 0 us
  Pallas kernels: 0 us -> 58.6 us
  waiting for transfers between devices: 50.5 us -> 0 us
  matrix products: 44.3 us -> 0 us
  between operations: 18.4 us -> 3.04 us
  other arithmetic: 15.3 us -> 0 us
  local copies, waits for them, and re-layouts: 17.2 us -> 6.12 us
    pallas_call x0 -> x1, Pallas kernels: none -> 58.6 us  [fused(): pl.pallas_call(functools.partial(block_kernel, (times, n, heads, rows, wi...]
    dot_general x13 -> x0, matrix products: 37.2 us -> none  [the longest x3 19.5 us: project_one_block(): jnp.dot(shaped, w_qkv, preferred_element_type=jnp.float32)]
    all_gather x3 -> x0, blocking collectives: 34.9 us -> none  [the longest x1 13.4 us: shards(): lax.all_gather(mod_piece, 'seq', axis=0, tiled=True)]
    all_gather x1 -> x0, waiting for transfers between devices: 34.1 us -> none  [shards(): lax.all_gather(own_heads, 'seq', axis=0, tiled=True)]
    psum x2 -> x0, blocking collectives: 19.1 us -> none  [the longest x1 9.59 us: shards(): lax.psum((jnp.sum(hidden, axis=1), jnp.sum(hidden * hidden, axis=1)), 'seq')]
    unnamed x3 -> x0, waiting for transfers between devices: 16.4 us -> none
    all_to_all x1 -> x0, blocking collectives: 13.3 us -> none  [shards(): lax.all_to_all(outputs, 'seq', split_axis=0, concat_axis=1, tiled=True)]
    sub x3 -> x0, matrix products: 7.14 us -> none  [attend_one_block(): raised = jnp.exp(scores - highest)]
  transfers between devices with their start and end apart: 3 -> 0, of which waited for: 2 -> 0; matrix products, arithmetic and copies ran while one was open for 3% -> 0% of each run, Pallas kernels for 0% -> 0%
where the time goes in v1:
time: 68.1 us; the launch traced here: 67.7 us
  Pallas kernels  58.6 us (86%)
  local copies, waits for them, and re-layouts  6.12 us (9%)
  between operations  3.04 us (4%)
    pallas_call x1, Pallas kernels, fused(): pl.pallas_call(functools.partial(block_kernel, (times, n, heads, rows, wi...  58.6 us
    unnamed x3, local copies, waits for them, and re-layouts  4.63 us
    pallas_call x1, local copies, waits for them, and re-layouts, fused(): pl.pallas_call(functools.partial(block_kernel, (times, n, heads, rows, wi...  1.5 us

profile of v1, /device:TPU:6, one launch (start us, length us, event | category | flops | bytes accessed | tf_op | source)
XLA Modules:
  0.0 67.7 jit_solution(13154743817233658111)
XLA Ops:
  1.3 1.5 %copy.12.start_ref = f32[96,64]{1,0:T(8,128)} copy(f32[96,64]{0,1:T(8,128)} %param.10) | data formatting | bytes 49152 | tf_op args[0]
  2.7 1.5 %copy.13.latents_ref = f32[1,96,64]{2,1,0:T(8,128)} copy(f32[1,96,64]{1,2,0:T(8,128)} %param.11) | data formatting | bytes 49152 | tf_op args[1]
  4.2 1.7 %copy.14.w_final_hbm = bf16[768,64]{1,0:T(8,128)(2,1)} copy(bf16[768,64]{0,1:T(8,128)(2,1)} %param.19) | data formatting | bytes 196608 | tf_op args[9]
  5.9 58.6 %shard_map.113 = (f32[1,96,64]{2,1,0:T(8,128)}, f32[1]{0:T(128)}) custom-call(s32[1]{0:T(128)S(6)} %copy.17.index_ref, f32[65]{0:T(128)} %sigmas_ref.1, f32[96,64]{1,0:T(8,128)} %copy.12.start_ref, f32[1,96,64]{2,1,0:T(8,128)} %copy.13.latents_ref, f32[2,512]{1,0:T(2,128)} %gains_ref.1, bf16[64,3072]{1,0:T(8,128)(2,1)} %w_embed_hbm.1, ...), custom_call_target="tpu_custom_call" | custom-call | flops 4831838208 | bytes 16777216 | tf_op jit(solution)/shard_map/pallas_call | solution.py:519
  64.5 1.5 %copy.15 = f32[1,96,64]{1,2,0:T(8,128)} copy(f32[1,96,64]{2,1,0:T(8,128)} %get-tuple-element.2) | data formatting | bytes 49152 | tf_op jit(solution)/shard_map/pallas_call | solution.py:519

commit v2 on v1

--- a/solution.py
+++ b/solution.py
@@ -207,7 +207,7 @@
     load_final.start()
     load_out.start()
 
-    state_out[...] = jnp.where(me_t == times - 1, start_ref[...], latents_ref[0]).astype(jnp.bfloat16)
+    state_out[...] = jnp.where(me_t == times - 1, start_ref[...], latents_ref[0]).T.astype(jnp.bfloat16)
 
     sigma_now = sigmas_ref[index_ref[0]]
     step_size = sigmas_ref[index_ref[0] + 1] - sigma_now
@@ -334,6 +334,10 @@
 
     gate, shift, scale = mod[2 * n + me], mod[3 * n + me], 1.0 + mod[4 * n + me]
     final = w_final[...]
+
+    def onto_final(x):
+        return lax.dot_general(x, final, (((1,), (1,)), ((), ())), preferred_element_type=jnp.float32)
+
     row = lax.broadcasted_iota(jnp.int32, (16, cols), 0)
 
     def high(x):
@@ -344,7 +348,7 @@
         high(scale),
         jnp.where(row == 1, scale - high(scale), jnp.where(row == 2, high(shift), shift - high(shift))),
     )
-    sides = jnp.dot(stacked.astype(jnp.bfloat16), final, preferred_element_type=jnp.float32)
+    sides = onto_final(stacked.astype(jnp.bfloat16))
     side_row = lax.broadcasted_iota(jnp.int32, (8, chan), 0)
     sides = jnp.where(
         side_row == 0,
@@ -395,9 +399,7 @@
         scaled = hidden * scale
         upper = scaled.astype(jnp.bfloat16)
         lower = (scaled - upper.astype(jnp.float32)).astype(jnp.bfloat16)
-        product = jnp.dot(upper, final, preferred_element_type=jnp.float32) + jnp.dot(
-            lower, final, preferred_element_type=jnp.float32
-        )
+        product = onto_final(upper) + onto_final(lower)
         stats = jnp.where(lane == 0, sums, jnp.where(lane == 1, square_sums, 0.0))
         return jnp.concatenate([product, stats], axis=1)
 
@@ -456,7 +458,7 @@
     for k in range(1, times):
         before = before + terms[k]
     change = jnp.concatenate([before[:, :chan], before[:, chan:]], axis=0)
-    updated = start_ref[...] + change
+    updated = start_ref[...] + change.T
     new_ref[0] = updated
     difference = updated - latents_ref[0]
     squares[me] = jnp.broadcast_to(jnp.sum(difference * difference), (8, 128))
@@ -516,10 +518,10 @@
     )
     dma = pltpu.SemaphoreType.DMA
     flops = 2 * rows * n * (width * heads * 3 * HD + n * heads * HD * cols)
-    return pl.pallas_call(
+    new_latents, error = pl.pallas_call(
         functools.partial(block_kernel, (times, n, heads, rows, width, chan)),
         out_shape=(
-            jax.ShapeDtypeStruct(latents.shape, wide),
+            jax.ShapeDtypeStruct((1, chan, rows), wide),
             jax.ShapeDtypeStruct((1,), wide),
         ),
         in_specs=[smem, smem, vmem, vmem, vmem, hbm, hbm, hbm, hbm, hbm],
@@ -529,7 +531,7 @@
             pltpu.VMEM(w_mod.shape, low),
             pltpu.VMEM((heads, width, 3 * HD), low),
             pltpu.VMEM(w_out.shape, low),
-            pltpu.VMEM(w_final.shape, low),
+            pltpu.VMEM((chan, cols), low),
             pltpu.VMEM((rows, chan), low),
             pltpu.VMEM((n, rows, chan), low),
             pltpu.VMEM((5 * n, 1, cols), wide),
@@ -561,7 +563,11 @@
             collective_id=0, has_side_effects=True, vmem_limit_bytes=56 * 2**20
         ),
         cost_estimate=pl.CostEstimate(flops=flops, bytes_accessed=16 * 2**20, transcendentals=0),
-    )(step_index, sigmas, window_start, latents, qk_gain, w_embed, w_mod, w_qkv, w_out, w_final)
+    )(
+        step_index, sigmas, window_start.T, jnp.swapaxes(latents, 1, 2), qk_gain,
+        w_embed, w_mod, w_qkv, w_out, w_final.T,
+    )
+    return jnp.swapaxes(new_latents, 1, 2), error
 
 
 def fits(times, n, args):

time: 68.1 us -> 63.3 us (0.930)
  local copies, waits for them, and re-layouts: 6.12 us -> 1.38 us
    unnamed x3 -> x1, local copies, waits for them, and re-layouts: 4.63 us -> 1.38 us
    pallas_call x1 -> x0, local copies, waits for them, and re-layouts: 1.5 us -> none  [fused(): pl.pallas_call(functools.partial(block_kernel, (times, n, heads, rows, wi...]
where the time goes in v2:
time: 63.3 us; the launch traced here: 63.1 us
  Pallas kernels  58.6 us (93%)
  between operations  3.05 us (5%)
  local copies, waits for them, and re-layouts  1.38 us (2%)
    pallas_call x1, Pallas kernels, fused(): pl.pallas_call(functools.partial(block_kernel, (times, n, heads, rows, wi...  58.6 us
    unnamed x1, local copies, waits for them, and re-layouts  1.38 us

profile of v2, /device:TPU:6, one launch (start us, length us, event | category | flops | bytes accessed | tf_op | source)
XLA Modules:
  0.0 63.1 jit_solution(595801729603274041)
XLA Ops:
  1.3 58.6 %shard_map.113 = (f32[1,64,96]{2,1,0:T(8,128)}, f32[1]{0:T(128)}) custom-call(s32[1]{0:T(128)S(6)} %copy.14.index_ref, f32[65]{0:T(128)} %sigmas_ref.1, f32[64,96]{1,0:T(8,128)} %bitcast.6, f32[1,64,96]{2,1,0:T(8,128)} %bitcast.7, f32[2,512]{1,0:T(2,128)} %gains_ref.1, bf16[64,3072]{1,0:T(8,128)(2,1)} %w_embed_hbm.1, bf16[256,3840]{1,0:T(8,128)(2,1)} %w_mod_hbm.1, ...), custom_call_target="tpu_custom_call" | custom-call | flops 4831838208 | bytes 16777216 | tf_op jit(solution)/shard_map/pallas_call | solution.py:521
  59.9 1.4 %copy.15 = f32[1,96,64]{1,2,0:T(8,128)} copy(f32[1,96,64]{1,2,0:T(8,128)} %bitcast.4) | data formatting | bytes 49152

commit v3 on v2

--- a/solution.py
+++ b/solution.py
@@ -171,12 +171,12 @@
 
 
 def block_kernel(
-    dims, index_ref, sigmas_ref, start_ref, latents_ref, gains_ref, w_embed_hbm, w_mod_hbm,
-    w_qkv_hbm, w_out_hbm, w_final_hbm, new_ref, error_ref,
-    w_embed, w_mod, w_qkv, w_out, w_final, state_out, state, mod, embedded, shaped, attended, total,
-    part_out, parts, terms, squares,
+    dims, index_ref, sigmas_ref, start_hbm, latents_hbm, gains_hbm, w_embed_hbm, w_mod_hbm,
+    w_qkv_hbm, w_out_hbm, w_final_hbm, new_hbm, error_ref,
+    start_ref, latents_ref, gains_ref, new_ref, w_embed, w_mod, w_qkv, w_out, w_final, state_out, state, mod, embedded, shaped, attended, total,
+    part_out, parts, stat_out, stats, sides, terms, squares,
     load_sem, qkv_sem, state_send, state_recv, mod_send, mod_recv, right_send, left_send, att_recv,
-    part_send, part_recv, term_send, term_recv, square_send, square_recv,
+    part_send, part_recv, stat_send, stat_recv, side_send, side_recv, term_send, term_recv, square_send, square_recv,
 ):
     times, n, heads, rows, width, chan = dims
     cols = width // n
@@ -198,6 +198,13 @@
     load_embed = pltpu.make_async_copy(w_embed_hbm, w_embed, load_sem.at[1])
     load_final = pltpu.make_async_copy(w_final_hbm, w_final, load_sem.at[2])
     load_out = pltpu.make_async_copy(w_out_hbm, w_out, load_sem.at[3])
+    small = [
+        pltpu.make_async_copy(start_hbm, start_ref, load_sem.at[4]),
+        pltpu.make_async_copy(latents_hbm.at[0], latents_ref, load_sem.at[5]),
+        pltpu.make_async_copy(gains_hbm, gains_ref, load_sem.at[6]),
+    ]
+    for load in small:
+        load.start()
     load_mod.start()
     load_embed.start()
     for h in range(heads):
@@ -207,7 +214,33 @@
     load_final.start()
     load_out.start()
 
-    state_out[...] = jnp.where(me_t == times - 1, start_ref[...], latents_ref[0]).T.astype(jnp.bfloat16)
+    half = rows // 2
+    for load in small:
+        load.wait()
+    own_state = jnp.where(me_t == times - 1, start_ref[...], latents_ref[...]).T
+    state_out[...] = jnp.concatenate([own_state[:half], own_state[half:]], axis=1).astype(jnp.bfloat16)
+
+    pl.semaphore_wait(barrier, len(peers))
+
+    def remote(source, target, send, recv, device):
+        return pltpu.make_async_remote_copy(
+            src_ref=source, dst_ref=target, send_sem=send, recv_sem=recv,
+            device_id=device, device_id_type=MESH,
+        )
+
+    def state_copy(slot, target):
+        return remote(
+            state_out, state.at[slot], state_send.at[target], state_recv.at[slot], (next_t, target)
+        )
+
+    for k in range(n):
+        state_copy(me, k).start()
+
+    def mod_copy(owner, k):
+        held = mod.at[pl.ds(owner * 5, 5)]
+        return remote(
+            held, held, mod_send.at[k], mod_recv.at[owner], (me_t, lax.rem(me + k, n))
+        )
 
     sigma_now = sigmas_ref[index_ref[0]]
     step_size = sigmas_ref[index_ref[0] + 1] - sigma_now
@@ -215,28 +248,6 @@
     angles = (1000.0 * sigma_now) * jnp.exp(place * (-math.log(10000.0) / (FREQ // 2)))
     features = jnp.concatenate([jnp.cos(angles), jnp.sin(angles)], axis=1).astype(jnp.bfloat16)
 
-    pl.semaphore_wait(barrier, len(peers))
-
-    def remote(source, target, send, recv, device):
-        return pltpu.make_async_remote_copy(
-            src_ref=source, dst_ref=target, send_sem=send, recv_sem=recv,
-            device_id=device, device_id_type=MESH,
-        )
-
-    def state_copy(slot, target):
-        return remote(
-            state_out, state.at[slot], state_send.at[target], state_recv.at[slot], (next_t, target)
-        )
-
-    for k in range(n):
-        state_copy(me, k).start()
-
-    def mod_copy(owner, k):
-        held = mod.at[pl.ds(owner * 5, 5)]
-        return remote(
-            held, held, mod_send.at[k], mod_recv.at[owner], (me_t, lax.rem(me + k, n))
-        )
-
     load_mod.wait()
     for i in range(5):
         piece = jnp.dot(
@@ -249,7 +260,9 @@
     load_embed.wait()
     for k in range(n):
         state_copy(k, 0).wait_recv()
-    state_low = state[...].reshape(all_rows, chan)
+    state_low = jnp.concatenate(
+        [state[k // 2, :, (k % 2) * chan : (k % 2 + 1) * chan] for k in range(2 * n)], axis=0
+    )
     sums = jnp.zeros((all_rows, 1), jnp.float32)
     for j in range(n):
         tile = jnp.dot(
@@ -287,6 +300,23 @@
             held, held, sems.at[slot], att_recv.at[slot], (me_t, me + 1 if right else me - 1)
         )
 
+    def collect(far, h):
+        @pl.when(me - far >= 0)
+        def _():
+            att_copy(me - far, h, True).wait_recv()
+
+            @pl.when(me < n - 1)
+            def _():
+                att_copy(me - far, h, True).start()
+
+        @pl.when(me + far < n)
+        def _():
+            att_copy(me + far, h, False).wait_recv()
+
+            @pl.when(me > 0)
+            def _():
+                att_copy(me + far, h, False).start()
+
     def one_head(h, carry):
         pltpu.make_async_copy(
             w_qkv_hbm.at[:, pl.ds(0, 3 * HD)], w_qkv.at[h], qkv_sem.at[h]
@@ -313,6 +343,10 @@
         def _():
             att_copy(me, h, False).start()
 
+        @pl.when(h >= 1)
+        def _():
+            collect(1, h - 1)
+
         return carry
 
     lax.fori_loop(0, heads, one_head, 0)
@@ -348,33 +382,30 @@
         high(scale),
         jnp.where(row == 1, scale - high(scale), jnp.where(row == 2, high(shift), shift - high(shift))),
     )
-    sides = onto_final(stacked.astype(jnp.bfloat16))
+    row_of = onto_final(stacked.astype(jnp.bfloat16))
     side_row = lax.broadcasted_iota(jnp.int32, (8, chan), 0)
-    sides = jnp.where(
+    row_of = jnp.where(
         side_row == 0,
-        sides[0:1] + sides[1:2],
-        jnp.where(side_row == 1, sides[2:3] + sides[3:4], 0.0),
-    )
-    sides = jnp.concatenate([sides, jnp.zeros((8, 128 - chan), jnp.float32)], axis=1)
+        row_of[0:1] + row_of[1:2],
+        jnp.where(side_row == 1, row_of[2:3] + row_of[3:4], 0.0),
+    )
+    sides[me] = jnp.concatenate([row_of, jnp.zeros((8, 128 - chan), jnp.float32)], axis=1)
+
+    def side_copy(source, k):
+        return remote(
+            sides.at[source], sides.at[source], side_send.at[k], side_recv.at[source],
+            (me_t, lax.rem(me + k, n)),
+        )
+
+    for k in range(1, n):
+        side_copy(me, k).start()
 
     def arrived(step, carry):
         far, h = step // heads + 1, lax.rem(step, heads)
 
-        @pl.when(me - far >= 0)
-        def _():
-            att_copy(me - far, h, True).wait_recv()
-
-            @pl.when(me < n - 1)
-            def _():
-                att_copy(me - far, h, True).start()
-
-        @pl.when(me + far < n)
-        def _():
-            att_copy(me + far, h, False).wait_recv()
-
-            @pl.when(me > 0)
-            def _():
-                att_copy(me + far, h, False).start()
+        @pl.when((far > 1) | (h == heads - 1))
+        def _():
+            collect(far, h)
 
         @pl.when(me - far >= 0)
         def _():
@@ -394,14 +425,16 @@
     def part_of(owner):
         at = pl.ds(pl.multiple_of(owner * rows, rows), rows)
         hidden = embedded[at, my_cols] + gate * total[at, :]
-        sums = jnp.sum(hidden, axis=1, keepdims=True)
-        square_sums = jnp.sum(hidden * hidden, axis=1, keepdims=True)
-        scaled = hidden * scale
+        middle = jnp.sum(hidden, axis=1, keepdims=True) / cols
+        centered = hidden - middle
+        square_sums = jnp.sum(centered * centered, axis=1, keepdims=True)
+        scaled = centered * scale
         upper = scaled.astype(jnp.bfloat16)
         lower = (scaled - upper.astype(jnp.float32)).astype(jnp.bfloat16)
         product = onto_final(upper) + onto_final(lower)
-        stats = jnp.where(lane == 0, sums, jnp.where(lane == 1, square_sums, 0.0))
-        return jnp.concatenate([product, stats], axis=1)
+        own_stats = jnp.where(lane == 0, middle, jnp.where(lane == 1, square_sums, 0.0))
+        both = jnp.concatenate([product, own_stats], axis=1).T
+        return both[:chan], both[chan : chan + 8]
 
     def part_copy(k, source, owner):
         return remote(
@@ -409,28 +442,48 @@
             (me_t, owner),
         )
 
+    def stat_copy(k, source, owner):
+        return remote(
+            stat_out.at[k - 1], stats.at[source], stat_send.at[k - 1], stat_recv.at[source],
+            (me_t, owner),
+        )
+
     for k in range(1, n):
         owner = lax.rem(me + k, n)
-        part_out[k - 1, :rows] = part_of(owner)
-        part_out[k - 1, rows:] = sides
+        product, own_stats = part_of(owner)
+        part_out[k - 1] = product.astype(jnp.bfloat16)
+        stat_out[k - 1] = own_stats
         part_copy(k, me, owner).start()
-    parts[me, :rows] = part_of(me)
-    parts[me, rows:] = sides
+        stat_copy(k, me, owner).start()
+    products, stats_of, sides_of = [None] * n, [None] * n, [None] * n
+    products[0], stats_of[0] = part_of(me)
+    sides_of[0] = sides[me].T
+    for k in range(1, n):
+        source = lax.rem(me + k, n)
+        side_copy(source, k).wait_recv()
+        sides_of[k] = sides[source].T
     for k in range(1, n):
         source = lax.rem(me + k, n)
         part_copy(k, source, source).wait_recv()
-    summed = parts[0]
-    for k in range(1, n):
-        summed = summed + parts[k]
-    average = summed[:rows, chan : chan + 1] / width
-    spread = summed[:rows, chan + 1 : chan + 2] / width - average * average
-    drift = (summed[:rows, :chan] - average * summed[rows : rows + 1, :chan]) * lax.rsqrt(
-        spread + epsilon
-    ) + summed[rows + 1 : rows + 2, :chan]
+        stat_copy(k, source, source).wait_recv()
+        products[k] = parts[source].astype(jnp.float32)
+        stats_of[k] = stats[source]
+    average = sum(held[0:1] for held in stats_of) / n
+    spread = sum(held[1:2] + cols * (held[0:1] - average) ** 2 for held in stats_of) / width
+    direct = sum(
+        product + side[:chan, 0:1] * (held[0:1] - average)
+        for product, side, held in zip(products, sides_of, stats_of)
+    )
+    drift = direct * lax.rsqrt(spread + epsilon) + sum(side[:chan, 1:2] for side in sides_of)
     increment = step_size * drift
-    half = rows // 2
-    packed = jnp.concatenate([increment[:half], increment[half:]], axis=1)
-    terms[me_t] = packed
+    spare = 128 - rows
+    folds = rows // spare
+    tail = chan // (folds + 1)
+    body = chan - tail
+    folded = jnp.concatenate(
+        [increment[body:, i * spare : (i + 1) * spare] for i in range(folds)], axis=0
+    )
+    terms[me_t] = jnp.concatenate([increment[:body], folded], axis=1)
 
     def term_copy(source, target):
         return remote(
@@ -452,15 +505,19 @@
 
         @pl.when(me_t - k < 0)
         def _():
-            terms[me_t - k + times] = jnp.zeros((half, 128), jnp.float32)
+            terms[me_t - k + times] = jnp.zeros((body, 128), jnp.float32)
 
     before = terms[0]
     for k in range(1, times):
         before = before + terms[k]
-    change = jnp.concatenate([before[:, :chan], before[:, chan:]], axis=0)
-    updated = start_ref[...] + change.T
-    new_ref[0] = updated
-    difference = updated - latents_ref[0]
+    unfolded = jnp.concatenate(
+        [before[i * tail : (i + 1) * tail, rows:] for i in range(folds)], axis=1
+    )
+    updated = start_ref[...] + jnp.concatenate([before[:, :rows], unfolded], axis=0)
+    new_ref[...] = updated
+    store = pltpu.make_async_copy(new_ref, new_hbm.at[0], load_sem.at[7])
+    store.start()
+    difference = updated - latents_ref[...]
     squares[me] = jnp.broadcast_to(jnp.sum(difference * difference), (8, 128))
 
     def square_copy(source, k):
@@ -477,6 +534,8 @@
     for k in range(1, n):
         mod_copy(me, k).wait_send()
         part_copy(k, me, lax.rem(me + k, n)).wait_send()
+        stat_copy(k, me, lax.rem(me + k, n)).wait_send()
+        side_copy(me, k).wait_send()
     for k in range(1, times):
 
         @pl.when(me_t + k < times)
@@ -503,6 +562,7 @@
     square_total = squares[0]
     for k in range(1, n):
         square_total = square_total + squares[k]
+    store.wait()
     error_ref[0] = jnp.max(square_total) / (all_rows * chan)
 
 
@@ -513,9 +573,7 @@
     heads = qk_gain.shape[1] // HD
     cols = width // n
     low, wide = jnp.bfloat16, jnp.float32
-    vmem, smem, hbm = (
-        pl.BlockSpec(memory_space=space) for space in (pltpu.VMEM, pltpu.SMEM, pl.ANY)
-    )
+    smem, hbm = pl.BlockSpec(memory_space=pltpu.SMEM), pl.BlockSpec(memory_space=pl.ANY)
     dma = pltpu.SemaphoreType.DMA
     flops = 2 * rows * n * (width * heads * 3 * HD + n * heads * HD * cols)
     new_latents, error = pl.pallas_call(
@@ -524,26 +582,33 @@
             jax.ShapeDtypeStruct((1, chan, rows), wide),
             jax.ShapeDtypeStruct((1,), wide),
         ),
-        in_specs=[smem, smem, vmem, vmem, vmem, hbm, hbm, hbm, hbm, hbm],
-        out_specs=(vmem, smem),
+        in_specs=[smem, smem, hbm, hbm, hbm, hbm, hbm, hbm, hbm, hbm],
+        out_specs=(hbm, smem),
         scratch_shapes=[
+            pltpu.VMEM((chan, rows), wide),
+            pltpu.VMEM((chan, rows), wide),
+            pltpu.VMEM(qk_gain.shape, wide),
+            pltpu.VMEM((chan, rows), wide),
             pltpu.VMEM(w_embed.shape, low),
             pltpu.VMEM(w_mod.shape, low),
             pltpu.VMEM((heads, width, 3 * HD), low),
             pltpu.VMEM(w_out.shape, low),
             pltpu.VMEM((chan, cols), low),
-            pltpu.VMEM((rows, chan), low),
-            pltpu.VMEM((n, rows, chan), low),
+            pltpu.VMEM((rows // 2, 2 * chan), low),
+            pltpu.VMEM((n, rows // 2, 2 * chan), low),
             pltpu.VMEM((5 * n, 1, cols), wide),
             pltpu.VMEM((rows * n, width), wide),
             pltpu.VMEM((rows * n, width), low),
             pltpu.VMEM((n * heads, rows * n, HD), low),
             pltpu.VMEM((rows * n, cols), wide),
-            pltpu.VMEM((n - 1, rows + 8, 128), wide),
-            pltpu.VMEM((n, rows + 8, 128), wide),
-            pltpu.VMEM((times, rows // 2, 128), wide),
+            pltpu.VMEM((n - 1, chan, rows), low),
+            pltpu.VMEM((n, chan, rows), low),
+            pltpu.VMEM((n - 1, 8, rows), wide),
+            pltpu.VMEM((n, 8, rows), wide),
             pltpu.VMEM((n, 8, 128), wide),
-            dma((4,)),
+            pltpu.VMEM((times, chan * rows // 128, 128), wide),
+            pltpu.VMEM((n, 8, 128), wide),
+            dma((8,)),
             dma((heads,)),
             dma((n,)),
             dma((n,)),
@@ -553,6 +618,10 @@
             dma((n * heads,)),
             dma((n * heads,)),
             dma((n - 1,)),
+            dma((n,)),
+            dma((n - 1,)),
+            dma((n,)),
+            dma((n,)),
             dma((n,)),
             dma((times,)),
             dma((times,)),
@@ -574,7 +643,7 @@
     rows, chan = args[0].shape
     cols = args[4].shape[1] // n
     small = rows * n * args[4].shape[1] <= 384 * 3072
-    return times > 2 and n > 1 and cols % 128 == 0 and rows % 32 == 0 and chan == 64 and small
+    return times > 2 and n > 1 and cols % 128 == 0 and rows in (64, 96) and chan == 64 and small
 
 
 def device_part(*args):

time: 63.3 us -> 60.9 us (0.962)
  Pallas kernels: 58.6 us -> 56.2 us
    pallas_call x1, Pallas kernels: 58.6 us -> 56.2 us  [fused(): pl.pallas_call(functools.partial(block_kernel, (times, n, heads, rows, wi...]
where the time goes in v3:
time: 60.9 us; the launch traced here: 60.6 us
  Pallas kernels  56.2 us (92%)
  between operations  3.05 us (5%)
  local copies, waits for them, and re-layouts  1.38 us (2%)
    pallas_call x1, Pallas kernels, fused(): pl.pallas_call(functools.partial(block_kernel, (times, n, heads, rows, wi...  56.2 us
    unnamed x1, local copies, waits for them, and re-layouts  1.38 us

profile of v3, /device:TPU:6, one launch (start us, length us, event | category | flops | bytes accessed | tf_op | source)
XLA Modules:
  0.0 60.6 jit_solution(14469001409746769270)
XLA Ops:
  1.3 56.2 %shard_map.113 = (f32[1,64,96]{2,1,0:T(8,128)}, f32[1]{0:T(128)}) custom-call(s32[1]{0:T(128)S(6)} %copy.14.index_ref, f32[65]{0:T(128)} %sigmas_ref.1, f32[64,96]{1,0:T(8,128)} %bitcast.6, f32[1,64,96]{2,1,0:T(8,128)} %bitcast.7, f32[2,512]{1,0:T(2,128)} %gains_hbm.1, bf16[64,3072]{1,0:T(8,128)(2,1)} %w_embed_hbm.1, bf16[256,3840]{1,0:T(8,128)(2,1)} %w_mod_hbm.1, ...), custom_call_target="tpu_custom_call" | custom-call | flops 4831838208 | bytes 16777216 | tf_op jit(solution)/shard_map/pallas_call | solution.py:579
  57.5 1.4 %copy.15 = f32[1,96,64]{1,2,0:T(8,128)} copy(f32[1,96,64]{1,2,0:T(8,128)} %bitcast.4) | data formatting | bytes 49152

commit v4 on v3

--- a/solution.py
+++ b/solution.py
@@ -220,8 +220,6 @@
     own_state = jnp.where(me_t == times - 1, start_ref[...], latents_ref[...]).T
     state_out[...] = jnp.concatenate([own_state[:half], own_state[half:]], axis=1).astype(jnp.bfloat16)
 
-    pl.semaphore_wait(barrier, len(peers))
-
     def remote(source, target, send, recv, device):
         return pltpu.make_async_remote_copy(
             src_ref=source, dst_ref=target, send_sem=send, recv_sem=recv,
@@ -233,8 +231,6 @@
             state_out, state.at[slot], state_send.at[target], state_recv.at[slot], (next_t, target)
         )
 
-    for k in range(n):
-        state_copy(me, k).start()
 
     def mod_copy(owner, k):
         held = mod.at[pl.ds(owner * 5, 5)]
@@ -254,6 +250,9 @@
             features, w_mod[:, i * cols : (i + 1) * cols], preferred_element_type=jnp.float32
         )
         mod[me * 5 + i] = piece[0:1]
+    pl.semaphore_wait(barrier, len(peers))
+    for k in range(n):
+        state_copy(me, k).start()
     for k in range(1, n):
         mod_copy(me, k).start()
 

time: 60.9 us -> 60.9 us (level)
  no operation moved by 1% of the time
where the time goes in v4:
time: 60.9 us; the launch traced here: 60.7 us
  Pallas kernels  56.3 us (92%)
  between operations  3.05 us (5%)
  local copies, waits for them, and re-layouts  1.38 us (2%)
    pallas_call x1, Pallas kernels, fused(): pl.pallas_call(functools.partial(block_kernel, (times, n, heads, rows, wi...  56.3 us
    unnamed x1, local copies, waits for them, and re-layouts  1.38 us

profile of v4, /device:TPU:6, one launch (start us, length us, event | category | flops | bytes accessed | tf_op | source)
XLA Modules:
  0.0 60.7 jit_solution(17058908077612733509)
XLA Ops:
  1.3 56.3 %shard_map.113 = (f32[1,64,96]{2,1,0:T(8,128)}, f32[1]{0:T(128)}) custom-call(s32[1]{0:T(128)S(6)} %copy.14.index_ref, f32[65]{0:T(128)} %sigmas_ref.1, f32[64,96]{1,0:T(8,128)} %bitcast.6, f32[1,64,96]{2,1,0:T(8,128)} %bitcast.7, f32[2,512]{1,0:T(2,128)} %gains_hbm.1, bf16[64,3072]{1,0:T(8,128)(2,1)} %w_embed_hbm.1, bf16[256,3840]{1,0:T(8,128)(2,1)} %w_mod_hbm.1, ...), custom_call_target="tpu_custom_call" | custom-call | flops 4831838208 | bytes 16777216 | tf_op jit(solution)/shard_map/pallas_call | solution.py:578
  57.6 1.4 %copy.15 = f32[1,96,64]{1,2,0:T(8,128)} copy(f32[1,96,64]{1,2,0:T(8,128)} %bitcast.4) | data formatting | bytes 49152
